TPU v7x, 32 devices: a whole 2x2x4 slice. The times are simulated.
32 devices in a mesh: morton: 16 (over z, y, x), sub: 2 (over core).
Axes of the slice: x: 2, y: 2, z: 4, core: 2. Of those that a mesh axis runs over, the one named last changes fastest.
Arguments:
- fine_multipole: bfloat16 [64, 32768], P(None, 'morton'), may hold values from -6 to 6
- coarse_multipole: bfloat16 [64, 5120], P(None, ('morton', 'sub')), may hold values from -6 to 6
- kernels: bfloat16 [316, 64, 64], P('sub'), may hold values from -0.0625 to 0.0625
- send_list: int32 [16, 16, 384], P('morton'), may hold values from 0 to 2047
- fine_source: int32 [316, 32768], P('sub', 'morton'), may hold values from 0 to 8192, as said below
- coarse_source: int32 [316, 5120], P('sub', 'morton'), may hold values from 0 to 5120, as said below
Outputs:
- fine_local: float32 [64, 32768], P(None, ('morton', 'sub'))
- coarse_local: float32 [64, 5120], P(None, ('morton', 'sub'))
Inputs may be any that keep to these rules, and one draw needn't show every extreme that they name: `fine_source`: values below 2048 name a box of the target's own Morton range m; the value 2048 + j * 384 + k names slot k of what range m + d_j sends to m, and that range always lies in 0 to 15; the value 2048 + 2 * 8 * 384 means no interaction. `coarse_source`: A value below 5120 names an upper-level source box; the value 5120 means no interaction.
All inputs are finite; a program needn't handle non-finite values.
Results may differ from a plain program's by a relative error of at most 0.0003.
Values may be sent and summed in bfloat16 or wider, within the bound.
A program may use at most 128 MiB of HBM per device.

v0:
```python
import math

import jax
import jax.numpy as jnp
from jax import lax
from jax.sharding import PartitionSpec as P


def passed_along(block, axis, distance):
    devices = range(lax.axis_size(axis))
    route = [(i - distance, i) for i in devices if i - distance in devices]
    return lax.ppermute(block, axis, route)


def translate(tables, columns, lists):
    block = math.gcd(lists.shape[1], 256)
    number = lists.shape[1] // block

    def one_block(index):
        chosen = lax.dynamic_slice_in_dim(lists, index * block, block, 1)
        gathered = jnp.take(columns, chosen, axis=1)
        return jnp.einsum("opq,qob->pb", tables, gathered, preferred_element_type=jnp.float32)

    blocks = lax.map(one_block, jnp.arange(number, dtype=jnp.int32))
    return jnp.transpose(blocks, (1, 0, 2)).reshape(tables.shape[1], lists.shape[1])


def per_device(fine_multipole, coarse_multipole, kernels, send_list, fine_source, coarse_source):
    width = fine_multipole.shape[0]
    blank = jnp.zeros((width, 1), jnp.bfloat16)
    reach_each = send_list.shape[1] // 2
    ghost_slots = send_list.shape[2]
    near_steps = [
        j - reach_each if j < reach_each else j - reach_each + 1 for j in range(2 * reach_each)
    ]
    send_rows = send_list[0]
    slot_count = send_rows.shape[1]
    outgoing = jnp.take(fine_multipole, send_rows.reshape(-1), axis=1).reshape(
        width, 2 * reach_each, slot_count
    )
    arrivals = []
    for j in range(2 * reach_each):
        arrivals.append(passed_along(outgoing[:, j], "morton", -near_steps[j]))
    received = jnp.stack(arrivals, axis=1)
    ghosts = received.reshape(width, 2 * reach_each * ghost_slots)
    extended = jnp.concatenate([fine_multipole, ghosts, blank], axis=1)
    fine_part = translate(kernels, extended, fine_source)
    gathered = lax.all_gather(coarse_multipole, ("morton", "sub"), axis=1, tiled=True)
    columns = jnp.concatenate([gathered, blank], axis=1)
    coarse_part = 0.5 * translate(kernels, columns, coarse_source)
    fine_local, coarse_local = (
        lax.psum_scatter(fine_part, "sub", scatter_dimension=1, tiled=True),
        lax.psum_scatter(coarse_part, "sub", scatter_dimension=1, tiled=True),
    )
    return (fine_local, coarse_local)


def solution(mesh):
    placed = (
        P(None, "morton"),
        P(None, ("morton", "sub")),
        P("sub", None, None),
        P("morton", None, None),
        P("sub", "morton"),
        P("sub", "morton"),
    )
    return jax.shard_map(
        per_device,
        mesh=mesh,
        in_specs=placed,
        out_specs=(P(None, ("morton", "sub")), P(None, ("morton", "sub"))),
        check_vma=False,
    )
```

profile of v0, /device:TPU:0, one launch (start us, length us, event | category | flops | bytes accessed | tf_op | source)
XLA Modules:
  0.0 1129.9 jit_solution(7438747328487859638)
XLA Ops:
  10.0 18.1 %gather_fusion.2 = bf16[6144,64]{1,0:T(8,128)(2,1)S(1)} fusion(bf16[64,2048]{0,1:T(8,128)(2,1)S(1)} %copy.41, s32[6144]{0:T(1024)S(1)} %broadcast_clamp_fusion), kind=kCustom, calls=%fused_computation.2 | custom fusion | bytes 1597440 | tf_op jit(solution)/shard_map/jit(_take)/gather | solution.py:38
  51.6 39.9 %all-gather = bf16[32,160,64]{1,2,0:T(8,128)(2,1)S(1)} all-gather(bf16[1,160,64]{1,2,0:T(8,128)(2,1)S(1)} %bitcast.156), channel_id=1, replica_groups=mesh['morton'=16,'sub'=2] {'morton','sub'}, dimensions={0}, use_global_device_ids=true | all-gather | bytes 675840 | tf_op jit(solution)/shard_map/all_gather | solution.py:48
  96.6 164.6 %while.21 = (s32[]{:T(128)}, f32[5,64,64]{1,2,0:T(8,128)S(1)}, s32[5]{0:T(128)S(1)}, s32[158,320]{1,0:T(8,128)}, bf16[64,5121]{0,1:T(8,128)(2,1)S(1)}, /*index=5...) while((s32[]{:T(128)}, f32[5,64,64]{1,2,0:T(8,128)S(1)}, s32[5]{0:T(128)S(1)}, ...), condition=%wide.region_4.5_spmd, body=%wide.region_3.4_spmd.sunk | while | flops 83555592 | bytes 8129319 | solution.py:24
  98.9 21.4 %gather_fusion.1 = bf16[10112,64]{1,0:T(8,128)(2,1)} fusion(bf16[64,5121]{0,1:T(8,128)(2,1)S(1)} %get-tuple-element.302, s32[10240]{0:T(1024)S(1)} %pad_clamp_fusion.5), kind=kCustom, calls=%fused_computation.1.clone.1 | custom fusion | bytes 2629120 | tf_op jit(solution)/shard_map/while/body/eval_jaxpr/jit(_take)/gather | solution.py:21
  131.8 21.4 %gather_fusion.1 = bf16[10112,64]{1,0:T(8,128)(2,1)} fusion(bf16[64,5121]{0,1:T(8,128)(2,1)S(1)} %get-tuple-element.302, s32[10240]{0:T(1024)S(1)} %pad_clamp_fusion.5), kind=kCustom, calls=%fused_computation.1.clone.1 | custom fusion | bytes 2629120 | tf_op jit(solution)/shard_map/while/body/eval_jaxpr/jit(_take)/gather | solution.py:21
  164.8 21.4 %gather_fusion.1 = bf16[10112,64]{1,0:T(8,128)(2,1)} fusion(bf16[64,5121]{0,1:T(8,128)(2,1)S(1)} %get-tuple-element.302, s32[10240]{0:T(1024)S(1)} %pad_clamp_fusion.5), kind=kCustom, calls=%fused_computation.1.clone.1 | custom fusion | bytes 2629120 | tf_op jit(solution)/shard_map/while/body/eval_jaxpr/jit(_take)/gather | solution.py:21
  197.7 21.4 %gather_fusion.1 = bf16[10112,64]{1,0:T(8,128)(2,1)} fusion(bf16[64,5121]{0,1:T(8,128)(2,1)S(1)} %get-tuple-element.302, s32[10240]{0:T(1024)S(1)} %pad_clamp_fusion.5), kind=kCustom, calls=%fused_computation.1.clone.1 | custom fusion | bytes 2629120 | tf_op jit(solution)/shard_map/while/body/eval_jaxpr/jit(_take)/gather | solution.py:21
  230.6 21.4 %gather_fusion.1 = bf16[10112,64]{1,0:T(8,128)(2,1)} fusion(bf16[64,5121]{0,1:T(8,128)(2,1)S(1)} %get-tuple-element.302, s32[10240]{0:T(1024)S(1)} %pad_clamp_fusion.5), kind=kCustom, calls=%fused_computation.1.clone.1 | custom fusion | bytes 2629120 | tf_op jit(solution)/shard_map/while/body/eval_jaxpr/jit(_take)/gather | solution.py:21
  314.8 803.0 %while.20 = (s32[]{:T(128)}, f32[8,64,256]{2,1,0:T(8,128)S(1)}, s32[8]{0:T(128)S(1)}, s32[158,2048]{1,0:T(8,128)}, bf16[64,8193]{0,1:T(8,128)(2,1)S(1)}, /*index...) while((s32[]{:T(128)}, f32[8,64,256]{2,1,0:T(8,128)S(1)}, s32[8]{0:T(128)S(1)}, ...), condition=%wide.region_1.2_spmd, body=%wide.region_0.1_spmd.sunk | while | flops 334222336 | bytes 28462760 | solution.py:24
  317.0 81.5 %gather_fusion = bf16[40448,64]{1,0:T(8,128)(2,1)} fusion(bf16[64,8193]{0,1:T(8,128)(2,1)S(1)} %get-tuple-element.272, s32[40960]{0:T(1024)S(1)} %pad_clamp_fusion.4), kind=kCustom, calls=%fused_computation.clone.1 | custom fusion | bytes 10516480 | tf_op jit(solution)/shard_map/while/body/eval_jaxpr/jit(_take)/gather | solution.py:21
  398.6 12.3 %copy.54 = bf16[158,256,64]{1,0,2:T(8,128)(2,1)} copy(bf16[158,256,64]{2,1,0:T(8,128)(2,1)} %bitcast.145) | data formatting | bytes 10354688 | tf_op jit(solution)/shard_map/while/body/eval_jaxpr/jit(_take)/gather | solution.py:21
  417.4 81.5 %gather_fusion = bf16[40448,64]{1,0:T(8,128)(2,1)} fusion(bf16[64,8193]{0,1:T(8,128)(2,1)S(1)} %get-tuple-element.272, s32[40960]{0:T(1024)S(1)} %pad_clamp_fusion.4), kind=kCustom, calls=%fused_computation.clone.1 | custom fusion | bytes 10516480 | tf_op jit(solution)/shard_map/while/body/eval_jaxpr/jit(_take)/gather | solution.py:21
  499.0 12.3 %copy.54 = bf16[158,256,64]{1,0,2:T(8,128)(2,1)} copy(bf16[158,256,64]{2,1,0:T(8,128)(2,1)} %bitcast.145) | data formatting | bytes 10354688 | tf_op jit(solution)/shard_map/while/body/eval_jaxpr/jit(_take)/gather | solution.py:21
  517.8 81.5 %gather_fusion = bf16[40448,64]{1,0:T(8,128)(2,1)} fusion(bf16[64,8193]{0,1:T(8,128)(2,1)S(1)} %get-tuple-element.272, s32[40960]{0:T(1024)S(1)} %pad_clamp_fusion.4), kind=kCustom, calls=%fused_computation.clone.1 | custom fusion | bytes 10516480 | tf_op jit(solution)/shard_map/while/body/eval_jaxpr/jit(_take)/gather | solution.py:21
  599.3 12.3 %copy.54 = bf16[158,256,64]{1,0,2:T(8,128)(2,1)} copy(bf16[158,256,64]{2,1,0:T(8,128)(2,1)} %bitcast.145) | data formatting | bytes 10354688 | tf_op jit(solution)/shard_map/while/body/eval_jaxpr/jit(_take)/gather | solution.py:21
  618.2 81.5 %gather_fusion = bf16[40448,64]{1,0:T(8,128)(2,1)} fusion(bf16[64,8193]{0,1:T(8,128)(2,1)S(1)} %get-tuple-element.272, s32[40960]{0:T(1024)S(1)} %pad_clamp_fusion.4), kind=kCustom, calls=%fused_computation.clone.1 | custom fusion | bytes 10516480 | tf_op jit(solution)/shard_map/while/body/eval_jaxpr/jit(_take)/gather | solution.py:21
  699.7 12.3 %copy.54 = bf16[158,256,64]{1,0,2:T(8,128)(2,1)} copy(bf16[158,256,64]{2,1,0:T(8,128)(2,1)} %bitcast.145) | data formatting | bytes 10354688 | tf_op jit(solution)/shard_map/while/body/eval_jaxpr/jit(_take)/gather | solution.py:21
  718.5 81.5 %gather_fusion = bf16[40448,64]{1,0:T(8,128)(2,1)} fusion(bf16[64,8193]{0,1:T(8,128)(2,1)S(1)} %get-tuple-element.272, s32[40960]{0:T(1024)S(1)} %pad_clamp_fusion.4), kind=kCustom, calls=%fused_computation.clone.1 | custom fusion | bytes 10516480 | tf_op jit(solution)/shard_map/while/body/eval_jaxpr/jit(_take)/gather | solution.py:21
  800.1 12.3 %copy.54 = bf16[158,256,64]{1,0,2:T(8,128)(2,1)} copy(bf16[158,256,64]{2,1,0:T(8,128)(2,1)} %bitcast.145) | data formatting | bytes 10354688 | tf_op jit(solution)/shard_map/while/body/eval_jaxpr/jit(_take)/gather | solution.py:21
  818.9 81.5 %gather_fusion = bf16[40448,64]{1,0:T(8,128)(2,1)} fusion(bf16[64,8193]{0,1:T(8,128)(2,1)S(1)} %get-tuple-element.272, s32[40960]{0:T(1024)S(1)} %pad_clamp_fusion.4), kind=kCustom, calls=%fused_computation.clone.1 | custom fusion | bytes 10516480 | tf_op jit(solution)/shard_map/while/body/eval_jaxpr/jit(_take)/gather | solution.py:21
  900.5 12.3 %copy.54 = bf16[158,256,64]{1,0,2:T(8,128)(2,1)} copy(bf16[158,256,64]{2,1,0:T(8,128)(2,1)} %bitcast.145) | data formatting | bytes 10354688 | tf_op jit(solution)/shard_map/while/body/eval_jaxpr/jit(_take)/gather | solution.py:21
  919.3 81.5 %gather_fusion = bf16[40448,64]{1,0:T(8,128)(2,1)} fusion(bf16[64,8193]{0,1:T(8,128)(2,1)S(1)} %get-tuple-element.272, s32[40960]{0:T(1024)S(1)} %pad_clamp_fusion.4), kind=kCustom, calls=%fused_computation.clone.1 | custom fusion | bytes 10516480 | tf_op jit(solution)/shard_map/while/body/eval_jaxpr/jit(_take)/gather | solution.py:21
  1019.7 81.5 %gather_fusion = bf16[40448,64]{1,0:T(8,128)(2,1)} fusion(bf16[64,8193]{0,1:T(8,128)(2,1)S(1)} %get-tuple-element.272, s32[40960]{0:T(1024)S(1)} %pad_clamp_fusion.4), kind=kCustom, calls=%fused_computation.clone.1 | custom fusion | bytes 10516480 | tf_op jit(solution)/shard_map/while/body/eval_jaxpr/jit(_take)/gather | solution.py:21
  1101.2 12.3 %copy.54 = bf16[158,256,64]{1,0,2:T(8,128)(2,1)} copy(bf16[158,256,64]{2,1,0:T(8,128)(2,1)} %bitcast.145) | data formatting | bytes 10354688 | tf_op jit(solution)/shard_map/while/body/eval_jaxpr/jit(_take)/gather | solution.py:21
  (173 shorter events, 203.7 us)
Async XLA Ops:
  7.2 1111.5 %reduce-scatter.5.cloned.1.call-start = ((), (), s32[]{:S(2)}) async-start(), calls=%async_computation.3 | async-start | bytes 245760 | tf_op jit(solution)/shard_map/reduce_scatter | solution.py:53
  30.6 231.5 %collective-permute-start = (bf16[64,384]{0,1:T(8,128)(2,1)}, bf16[64,384]{0,1:T(8,128)(2,1)}, u32[]{:S(2)}, u32[]{:S(2)}) collective-permute-start(bf16[64,384]{0,1:T(8,128)(2,1)} %get-tuple-element.165), channel_id=1, source_target_pairs={{0,16},{2,18},{4,20},{6,22},{8,24},{10,26},{12,28},{14,30},{1,17},... | collective-permute-start | bytes 147464 | tf_op jit(solution)/shard_map/ppermute | solution.py:12
  37.3 227.0 %collective-permute-start.1 = (bf16[64,384]{0,1:T(8,128)(2,1)}, bf16[64,384]{0,1:T(8,128)(2,1)}, u32[]{:S(2)}, u32[]{:S(2)}) collective-permute-start(bf16[64,384]{0,1:T(8,128)(2,1)} %get-tuple-element.164), channel_id=1, source_target_pairs={{0,14},{2,16},{4,18},{6,20},{8,22},{10,24},{12,26},{14,28},{16,30}... | collective-permute-start | bytes 147464 | tf_op jit(solution)/shard_map/ppermute | solution.py:12
  43.3 223.3 %collective-permute-start.2 = (bf16[64,384]{0,1:T(8,128)(2,1)}, bf16[64,384]{0,1:T(8,128)(2,1)}, u32[]{:S(2)}, u32[]{:S(2)}) collective-permute-start(bf16[64,384]{0,1:T(8,128)(2,1)} %get-tuple-element.163), channel_id=1, source_target_pairs={{0,12},{2,14},{4,16},{6,18},{8,20},{10,22},{12,24},{14,26},{16,28}... | collective-permute-start | bytes 147464 | tf_op jit(solution)/shard_map/ppermute | solution.py:12
  45.2 225.5 %collective-permute-start.3 = (bf16[64,384]{0,1:T(8,128)(2,1)}, bf16[64,384]{0,1:T(8,128)(2,1)}, u32[]{:S(2)}, u32[]{:S(2)}) collective-permute-start(bf16[64,384]{0,1:T(8,128)(2,1)} %get-tuple-element.162), channel_id=1, source_target_pairs={{0,10},{2,12},{4,14},{6,16},{8,18},{10,20},{12,22},{14,24},{16,26}... | collective-permute-start | bytes 147464 | tf_op jit(solution)/shard_map/ppermute | solution.py:12
  47.1 225.8 %collective-permute-start.4 = (bf16[64,384]{0,1:T(8,128)(2,1)}, bf16[64,384]{0,1:T(8,128)(2,1)}, u32[]{:S(2)}, u32[]{:S(2)}) collective-permute-start(bf16[64,384]{0,1:T(8,128)(2,1)} %get-tuple-element.161), channel_id=1, source_target_pairs={{0,8},{2,10},{4,12},{6,14},{8,16},{10,18},{12,20},{14,22},{16,24},... | collective-permute-start | bytes 147464 | tf_op jit(solution)/shard_map/ppermute | solution.py:12
  96.6 165.5 %copy-start.9 = (bf16[64,384]{0,1:T(8,128)(2,1)S(1)}, bf16[64,384]{0,1:T(8,128)(2,1)}, u32[]{:S(2)}) copy-start(bf16[64,384]{0,1:T(8,128)(2,1)} %get-tuple-element.160) | copy-start | bytes 147460
  96.6 167.7 %copy-start.8 = (bf16[64,384]{0,1:T(8,128)(2,1)S(1)}, bf16[64,384]{0,1:T(8,128)(2,1)}, u32[]{:S(2)}) copy-start(bf16[64,384]{0,1:T(8,128)(2,1)} %get-tuple-element.159) | copy-start | bytes 147460
  96.6 170.0 %copy-start.7 = (bf16[64,384]{0,1:T(8,128)(2,1)S(1)}, bf16[64,384]{0,1:T(8,128)(2,1)}, u32[]{:S(2)}) copy-start(bf16[64,384]{0,1:T(8,128)(2,1)} %get-tuple-element.158) | copy-start | bytes 147460
  96.6 174.1 %copy-start.6 = (bf16[64,384]{0,1:T(8,128)(2,1)S(1)}, bf16[64,384]{0,1:T(8,128)(2,1)}, u32[]{:S(2)}) copy-start(bf16[64,384]{0,1:T(8,128)(2,1)} %get-tuple-element.157) | copy-start | bytes 147460
  96.6 176.4 %copy-start.5 = (bf16[64,384]{0,1:T(8,128)(2,1)S(1)}, bf16[64,384]{0,1:T(8,128)(2,1)}, u32[]{:S(2)}) copy-start(bf16[64,384]{0,1:T(8,128)(2,1)} %get-tuple-element.156) | copy-start | bytes 147460
  96.6 178.6 %copy-start.4 = (bf16[64,384]{0,1:T(8,128)(2,1)S(1)}, bf16[64,384]{0,1:T(8,128)(2,1)}, u32[]{:S(2)}) copy-start(bf16[64,384]{0,1:T(8,128)(2,1)} %get-tuple-element.155) | copy-start | bytes 147460
  262.0 861.1 %reduce-scatter.3.cloned.1.call-start = ((), (), s32[]{:S(2)}) async-start(), calls=%async_computation.2 | async-start | bytes 786432 | tf_op jit(solution)/shard_map/reduce_scatter | solution.py:52
  262.1 13.1 %collective-permute-start.5 = (bf16[64,384]{0,1:T(8,128)(2,1)S(1)}, bf16[64,384]{0,1:T(8,128)(2,1)S(1)}, u32[]{:S(2)}, u32[]{:S(2)}) collective-permute-start(bf16[64,384]{0,1:T(8,128)(2,1)S(1)} %copy-done.9), channel_id=1, source_target_pairs={{0,6},{2,8},{4,10},{6,12},{8,14},{10,16},{12,18},{14,20},{16,22},{... | collective-permute-start | bytes 147464 | tf_op jit(solution)/shard_map/ppermute | solution.py:12
  264.3 12.2 %collective-permute-start.6 = (bf16[64,384]{0,1:T(8,128)(2,1)S(1)}, bf16[64,384]{0,1:T(8,128)(2,1)S(1)}, u32[]{:S(2)}, u32[]{:S(2)}) collective-permute-start(bf16[64,384]{0,1:T(8,128)(2,1)S(1)} %copy-done.8), channel_id=1, source_target_pairs={{0,4},{2,6},{4,8},{6,10},{8,12},{10,14},{12,16},{14,18},{16,20},{1... | collective-permute-start | bytes 147464 | tf_op jit(solution)/shard_map/ppermute | solution.py:12
  266.6 11.3 %collective-permute-start.7 = (bf16[64,384]{0,1:T(8,128)(2,1)S(1)}, bf16[64,384]{0,1:T(8,128)(2,1)S(1)}, u32[]{:S(2)}, u32[]{:S(2)}) collective-permute-start(bf16[64,384]{0,1:T(8,128)(2,1)S(1)} %copy-done.7), channel_id=1, source_target_pairs={{0,2},{2,4},{4,6},{6,8},{8,10},{10,12},{12,14},{14,16},{16,18},{18... | collective-permute-start | bytes 147464 | tf_op jit(solution)/shard_map/ppermute | solution.py:12
  270.7 8.5 collective-permute-start.8
  273.0 7.6 collective-permute-start.9
  275.2 9.2 collective-permute-start.10
  276.6 9.8 collective-permute-start.11
  277.9 11.3 %collective-permute-start.12 = (bf16[64,384]{0,1:T(8,128)(2,1)S(1)}, bf16[64,384]{0,1:T(8,128)(2,1)S(1)}, u32[]{:S(2)}, u32[]{:S(2)}) collective-permute-start(bf16[64,384]{0,1:T(8,128)(2,1)S(1)} %copy-done.2), channel_id=1, source_target_pairs={{10,0},{12,2},{14,4},{16,6},{18,8},{20,10},{22,12},{24,14},{26,16}... | collective-permute-start | bytes 147464 | tf_op jit(solution)/shard_map/ppermute | solution.py:12
  279.2 13.1 %collective-permute-start.13 = (bf16[64,384]{0,1:T(8,128)(2,1)S(1)}, bf16[64,384]{0,1:T(8,128)(2,1)S(1)}, u32[]{:S(2)}, u32[]{:S(2)}) collective-permute-start(bf16[64,384]{0,1:T(8,128)(2,1)S(1)} %copy-done.1), channel_id=1, source_target_pairs={{12,0},{14,2},{16,4},{18,6},{20,8},{22,10},{24,12},{26,14},{28,16}... | collective-permute-start | bytes 147464 | tf_op jit(solution)/shard_map/ppermute | solution.py:12
  280.6 14.3 %collective-permute-start.14 = (bf16[64,384]{0,1:T(8,128)(2,1)S(1)}, bf16[64,384]{0,1:T(8,128)(2,1)S(1)}, u32[]{:S(2)}, u32[]{:S(2)}) collective-permute-start(bf16[64,384]{0,1:T(8,128)(2,1)S(1)} %get-tuple-element.151), channel_id=1, source_target_pairs={{14,0},{16,2},{18,4},{20,6},{22,8},{24,10},{26,12},{28,14},{30,16}... | collective-permute-start | bytes 147464 | tf_op jit(solution)/shard_map/ppermute | solution.py:12
  284.4 20.4 %collective-permute-start.15 = (bf16[64,384]{0,1:T(8,128)(2,1)S(1)}, bf16[64,384]{0,1:T(8,128)(2,1)S(1)}, u32[]{:S(2)}, u32[]{:S(2)}) collective-permute-start(bf16[64,384]{0,1:T(8,128)(2,1)S(1)} %get-tuple-element.150), channel_id=1, source_target_pairs={{16,0},{18,2},{20,4},{22,6},{24,8},{26,10},{28,12},{30,14},{17,1},... | collective-permute-start | bytes 147464 | tf_op jit(solution)/shard_map/ppermute | solution.py:12
  (5 other events, 71.9 us)
Sparse Core Ops, SparseCore 0:
  262.1 4.6 reduce-scatter.4
  1118.8 4.2 reduce-scatter.2
where the time goes:
time: 1130 us
  local copies, waits for them, and re-layouts  933 us (83%)
  matrix products  49 us (4%)
  blocking collectives  39.9 us (4%)
  starting transfers between devices  34.9 us (3%)
  other arithmetic  25.7 us (2%)
  waiting for transfers between devices  24.3 us (2%)
  between operations  14.6 us (1%)
    gather x26, local copies, waits for them, and re-layouts, one_block(): gathered = jnp.take(columns, chosen, axis=1)  888 us
    dot_general x13, matrix products, one_block(): jnp.einsum('opq,qob->pb', tables, gathered, preferred_element_type=jnp.fl...  49 us
    all_gather x1, blocking collectives, per_device(): lax.all_gather(coarse_multipole, ('morton', 'sub'), axis=1, tiled=True)  39.9 us
    ppermute x16, starting transfers between devices, passed_along(): return lax.ppermute(block, axis, route)  34.8 us
  transfers between devices with their start and end apart: 18, of which 7 were waited for; matrix products, arithmetic and copies ran while one was open for 87% of the time, Pallas kernels for 0%

commit v1 on v0

v1 whole, which is shorter than its diff:
```python
import functools
import math

import jax
import jax.numpy as jnp
from jax import lax
from jax.experimental import pallas as pl
from jax.experimental.pallas import tpu as pltpu
from jax.sharding import PartitionSpec as P

GROUP = 4
BATCH = 8
BLANK = 16


def passed_along(block, axis, distance):
    devices = range(lax.axis_size(axis))
    route = [(i - distance, i) for i in devices if i - distance in devices]
    return lax.ppermute(block, axis, route)


def gather_multiply(targets, chunk, steps, offset_ref, index_ref, table_ref, kernel_ref, out_ref, held_ref):
    step = pl.program_id(0)
    width = out_ref.shape[1]

    @pl.when(step == 0)
    def _():
        out_ref[...] = jnp.zeros_like(out_ref)
        held_ref[...] = jnp.zeros_like(held_ref)

    left = lax.broadcasted_iota(jnp.int32, (1, 2 * width), 1) < width

    offsets = [offset_ref[t] for t in range(BATCH)]

    def product(rows):
        lhs = jnp.concatenate([held_ref[pair, rows, :] for pair in range(GROUP // 2)], axis=1)
        return jnp.dot(
            lhs.astype(jnp.bfloat16), kernel_ref[0], preferred_element_type=jnp.float32
        )

    def fetch(indices, batch):
        rows = []
        for pair in range(GROUP // 2):
            for t in range(BATCH):
                spot = 2 * pair * chunk + batch * BATCH
                first = table_ref[indices.at[pl.ds(spot, BATCH)][offsets[t]]]
                second = table_ref[indices.at[pl.ds(spot + chunk, BATCH)][offsets[t]]]
                rows.append(jnp.where(left, first, second))
        return rows

    def keep(base, batch, rows):
        for pair in range(GROUP // 2):
            for t in range(BATCH):
                held_ref[pair, pl.ds(base + (batch * BATCH + t), 1), :] = rows[pair * BATCH + t]

    @pl.when(step < steps)
    def _():
        @pl.loop(0, targets // chunk)
        def _(c):
            base = pl.multiple_of(c * chunk, chunk)
            rows = pl.ds(base, chunk)
            done = product(rows)
            indices = index_ref.at[0, c, 0]
            pending = fetch(indices, 0)
            for batch in range(1, chunk // BATCH):
                coming = fetch(indices, batch)
                keep(base, batch - 1, pending)
                pending = coming
            keep(base, chunk // BATCH - 1, pending)
            out_ref[rows, :] += done

    @pl.when(step == steps)
    def _():
        @pl.loop(0, targets // chunk)
        def _(c):
            rows = pl.ds(pl.multiple_of(c * chunk, chunk), chunk)
            out_ref[rows, :] += product(rows)


def translate(tables, table, lists):
    offsets, width, _ = tables.shape
    targets = lists.shape[1]
    chunk = math.gcd(targets, 64)
    steps = -(-offsets // GROUP)
    weights = jnp.transpose(tables, (0, 2, 1))
    weights = jnp.pad(weights, ((0, steps * GROUP - offsets), (0, 0), (0, 0)))
    weights = weights.reshape(steps, GROUP * width, width)
    parts = targets // chunk
    index = jnp.transpose(lists.reshape(steps, GROUP, parts, chunk), (0, 2, 1, 3))
    index = index.reshape(steps, parts, 1, GROUP * chunk)
    return pl.pallas_call(
        functools.partial(gather_multiply, targets, chunk, steps),
        grid=(steps + 1,),
        out_shape=jax.ShapeDtypeStruct((targets, width), jnp.float32),
        in_specs=[
            pl.BlockSpec(memory_space=pltpu.SMEM),
            pl.BlockSpec(
                (1, parts, 1, GROUP * chunk),
                lambda i: (jnp.minimum(i, steps - 1), 0, 0, 0),
                memory_space=pltpu.SMEM,
            ),
            pl.BlockSpec(
                table.shape, lambda i: (0, 0, 0), pipeline_mode=pl.Buffered(1)
            ),
            pl.BlockSpec(
                (1, GROUP * width, width), lambda i: (jnp.maximum(i - 1, 0), 0, 0)
            ),
        ],
        out_specs=pl.BlockSpec((targets, width), lambda i: (0, 0)),
        scratch_shapes=[pltpu.VMEM((GROUP // 2, targets, 2 * width), jnp.float32)],
        compiler_params=pltpu.CompilerParams(
            vmem_limit_bytes=48 * 1024 * 1024, dimension_semantics=("arbitrary",)
        ),
    )(jnp.arange(BATCH, dtype=jnp.int32), index, table, weights)


def per_device(fine_multipole, coarse_multipole, kernels, send_list, fine_source, coarse_source):
    width = fine_multipole.shape[0]
    reach_each = send_list.shape[1] // 2
    ghost_slots = send_list.shape[2]
    near_steps = [
        j - reach_each if j < reach_each else j - reach_each + 1 for j in range(2 * reach_each)
    ]
    own = jnp.transpose(fine_multipole)
    outgoing = jnp.take(own, send_list[0].reshape(-1), axis=0, mode="clip").reshape(
        2 * reach_each, ghost_slots, width
    )
    arrivals = [
        passed_along(outgoing[j], "morton", -near_steps[j]) for j in range(2 * reach_each)
    ]
    coarse = lax.all_gather(
        jnp.transpose(coarse_multipole), ("morton", "sub"), axis=0, tiled=True
    )
    blank = jnp.zeros((BLANK, width), jnp.bfloat16)
    rows = jnp.concatenate([own, *arrivals, blank, coarse, blank], axis=0)
    rows = rows.astype(jnp.float32)
    table = jnp.concatenate([rows, rows], axis=1)[:, None, :]
    no_source = own.shape[0] + 2 * reach_each * ghost_slots
    fine_half = fine_source.shape[1] // 2
    coarse_half = coarse_source.shape[1] // 2
    coarse_index = coarse_source + (no_source + BLANK)
    lists = jnp.concatenate(
        [
            fine_source[:, :fine_half],
            coarse_index[:, :coarse_half],
            fine_source[:, fine_half:],
            coarse_index[:, coarse_half:],
        ],
        axis=1,
    )
    extra = -lists.shape[0] % GROUP
    lists = jnp.pad(lists, ((0, extra), (0, 0)), constant_values=no_source)
    part = translate(kernels, table, lists)
    local = lax.psum_scatter(part, "sub", scatter_dimension=0, tiled=True)
    local = jnp.transpose(local)
    return local[:, :fine_half], 0.5 * local[:, fine_half:]


def solution(mesh):
    placed = (
        P(None, "morton"),
        P(None, ("morton", "sub")),
        P("sub", None, None),
        P("morton", None, None),
        P("sub", "morton"),
        P("sub", "morton"),
    )
    return jax.shard_map(
        per_device,
        mesh=mesh,
        in_specs=placed,
        out_specs=(P(None, ("morton", "sub")), P(None, ("morton", "sub"))),
        check_vma=False,
    )
```

time: 1130 us -> 443 us (0.39)
  local copies, waits for them, and re-layouts: 933 us -> 51.8 us
  Pallas kernels: 0 us -> 268 us
  matrix products: 49 us -> 0 us
  other arithmetic: 25.7 us -> 4.58 us
    gather x27 -> x1, local copies, waits for them, and re-layouts: 907 us -> 18.1 us  [per_device(): jnp.take(own, send_list[0].reshape(-1), axis=0, mode='clip')]
    pallas_call x0 -> x1, Pallas kernels: none -> 268 us  [translate(): pl.pallas_call(functools.partial(gather_multiply, targets, chunk, steps),...]
    dot_general x13 -> x0, matrix products: 49 us -> none  [one_block(): jnp.einsum('opq,qob->pb', tables, gathered, preferred_element_type=jnp.fl...]
    and x14 -> x0, other arithmetic: 13.5 us -> none  [the longest x13 12.7 us: one_block(): gathered = jnp.take(columns, chosen, axis=1)]
  transfers between devices with their start and end apart: 18 -> 17, of which waited for: 7 -> 8; matrix products, arithmetic and copies ran while one was open for 87% -> 6% of each run, Pallas kernels for 0% -> 0%
where the time goes in v1:
time: 443 us; the launch traced here: 442 us
  Pallas kernels  268 us (60%)
  local copies, waits for them, and re-layouts  51.8 us (12%)
  blocking collectives  39.9 us (9%)
  starting transfers between devices  34.6 us (8%)
  waiting for transfers between devices  28.4 us (6%)
  between operations  14.5 us (3%)
  other arithmetic  4.58 us (1%)
    pallas_call x1, Pallas kernels, translate(): pl.pallas_call(functools.partial(gather_multiply, targets, chunk, steps),...  268 us
    all_gather x1, blocking collectives, per_device(): lax.all_gather(jnp.transpose(coarse_multipole), ('morton', 'sub'), axis=0...  39.9 us
    ppermute x16, starting transfers between devices, passed_along(): return lax.ppermute(block, axis, route)  34.6 us
    ppermute x16, waiting for transfers between devices, passed_along(): return lax.ppermute(block, axis, route)  23 us
    gather x1, local copies, waits for them, and re-layouts, per_device(): jnp.take(own, send_list[0].reshape(-1), axis=0, mode='clip')  18.1 us
    unnamed x51, local copies, waits for them, and re-layouts  15.4 us
  transfers between devices with their start and end apart: 17, of which 8 were waited for; matrix products, arithmetic and copies ran while one was open for 6% of the time, Pallas kernels for 0%

profile of v1, /device:TPU:0, one launch (start us, length us, event | category | flops | bytes accessed | tf_op | source)
XLA Modules:
  0.0 441.6 jit_solution(5279441129082901385)
XLA Ops:
  9.2 18.1 %gather_fusion = bf16[6144,64]{1,0:T(8,128)(2,1)S(1)} fusion(bf16[2048,64]{1,0:T(8,128)(2,1)S(1)} %bitcast.12, s32[6144]{0:T(1024)S(1)} %broadcast_clamp_fusion), kind=kCustom, calls=%fused_computation | custom fusion | bytes 1597440 | tf_op jit(solution)/shard_map/jit(_take)/gather | solution.py:125
  28.4 6.6 %collective-permute-start = (bf16[384,64]{1,0:T(8,128)(2,1)}, bf16[384,64]{1,0:T(8,128)(2,1)}, u32[]{:S(2)}, u32[]{:S(2)}) collective-permute-start(bf16[384,64]{1,0:T(8,128)(2,1)} %get-tuple-element.23), channel_id=1, source_target_pairs={{0,16},{2,18},{4,20},{6,22},{8,24},{10,26},{12,28},{14,30},{1,17},... | collective-permute-start | bytes 147464 | tf_op jit(solution)/shard_map/ppermute | solution.py:19
  34.9 6.0 %collective-permute-start.1 = (bf16[384,64]{1,0:T(8,128)(2,1)}, bf16[384,64]{1,0:T(8,128)(2,1)}, u32[]{:S(2)}, u32[]{:S(2)}) collective-permute-start(bf16[384,64]{1,0:T(8,128)(2,1)} %get-tuple-element.22), channel_id=1, source_target_pairs={{0,14},{2,16},{4,18},{6,20},{8,22},{10,24},{12,26},{14,28},{16,30}... | collective-permute-start | bytes 147464 | tf_op jit(solution)/shard_map/ppermute | solution.py:19
  40.9 1.9 collective-permute-start.2
  42.9 1.9 collective-permute-start.3
  44.8 1.9 collective-permute-start.4
  47.5 39.9 %all-gather = bf16[32,160,64]{1,2,0:T(8,128)(2,1)S(1)} all-gather(bf16[1,160,64]{1,2,0:T(8,128)(2,1)S(1)} %bitcast.19), channel_id=1, replica_groups=mesh['morton'=16,'sub'=2] {'morton','sub'}, dimensions={0}, use_global_device_ids=true | all-gather | bytes 675840 | tf_op jit(solution)/shard_map/all_gather | solution.py:131
  87.7 1.5 copy.22
  91.1 2.6 reshape.47
  93.7 2.4 copy.20
  96.2 4.2 reshape.48.index_ref
  100.4 6.8 %copy.26 = bf16[158,64,64]{2,1,0:T(8,128)(2,1)} copy(bf16[158,64,64]{0,1,2:T(8,128)(2,1)} %bitcast.16) | data formatting | bytes 2588672
  107.3 2.6 pad.9.clone
  112.2 2.0 collective-permute-start.6
  115.1 2.6 collective-permute-start.7
  130.8 1.6 collective-permute-done.10
  133.7 2.2 collective-permute-done.11
  136.0 3.0 collective-permute-done.12
  139.0 2.7 collective-permute-done.13
  141.7 2.8 collective-permute-done.14
  144.5 9.7 %collective-permute-done.15 = bf16[384,64]{1,0:T(8,128)(2,1)S(1)} collective-permute-done((bf16[384,64]{1,0:T(8,128)(2,1)S(1)}, bf16[384,64]{1,0:T(8,128)(2,1)S(1)}, u32[]{:S(2)}, u32[]{:S(2)}) %collective-permute-start.15) | collective-permute-done | bytes 49184 | tf_op jit(solution)/shard_map/ppermute | solution.py:19
  154.4 3.7 maximum_convert_fusion
  158.1 267.7 %shard_map.77 = f32[2368,64]{1,0:T(8,128)} custom-call(s32[8]{0:T(128)S(1)} %iota.3.offset_ref, s32[40,37,1,256]{3,2,1,0:T(1,128)S(1)} %reshape.48.index_ref, f32[13344,1,128]{2,1,0:T(1,128)} %bitcast.13, bf16[40,256,64]{2,1,0:T(8,128)(2,1)S(1)} %bitcast.11), custom_call_target="tpu_custom_call" | custom-call | tf_op jit(solution)/shard_map/pallas_call | solution.py:91
  425.8 5.4 %reduce-scatter.2.cloned.1.call-done = f32[1184,64]{1,0:T(8,128)} async-done(((f32[2368,64]{1,0:T(8,128)}), f32[1184,64]{1,0:T(8,128)}) %reduce-scatter.2.cloned.1.call-update) | async-done | bytes 303120 | tf_op jit(solution)/shard_map/reduce_scatter | solution.py:154
  (83 shorter events, 27.2 us)
Async XLA Ops:
  7.2 424.0 %reduce-scatter.2.cloned.1.call-start = ((), (), s32[]{:S(2)}) async-start(), calls=%async_computation.1 | async-start | bytes 1818624 | tf_op jit(solution)/shard_map/reduce_scatter | solution.py:154
  27.3 20.3 %copy-start.13 = (bf16[64,160]{1,0:T(8,128)(2,1)S(1)}, bf16[64,160]{1,0:T(8,128)(2,1)}, u32[]{:S(2)}) copy-start(bf16[64,160]{1,0:T(8,128)(2,1)} %param.7) | copy-start | bytes 61444
  27.3 60.2 %copy-start.2 = (s32[158,2048]{1,0:T(8,128)S(1)}, s32[158,2048]{1,0:T(8,128)}, u32[]{:S(2)}) copy-start(s32[158,2048]{1,0:T(8,128)} %param.10) | copy-start | bytes 3883012
  27.3 60.2 %copy-start.3 = (s32[158,320]{1,0:T(8,128)S(1)}, s32[158,320]{1,0:T(8,128)}, u32[]{:S(2)}) copy-start(s32[158,320]{1,0:T(8,128)} %param.11) | copy-start | bytes 606724
  28.4 81.5 %collective-permute-start = (bf16[384,64]{1,0:T(8,128)(2,1)}, bf16[384,64]{1,0:T(8,128)(2,1)}, u32[]{:S(2)}, u32[]{:S(2)}) collective-permute-start(bf16[384,64]{1,0:T(8,128)(2,1)} %get-tuple-element.23), channel_id=1, source_target_pairs={{0,16},{2,18},{4,20},{6,22},{8,24},{10,26},{12,28},{14,30},{1,17},... | collective-permute-start | bytes 147464 | tf_op jit(solution)/shard_map/ppermute | solution.py:19
  34.9 77.2 %collective-permute-start.1 = (bf16[384,64]{1,0:T(8,128)(2,1)}, bf16[384,64]{1,0:T(8,128)(2,1)}, u32[]{:S(2)}, u32[]{:S(2)}) collective-permute-start(bf16[384,64]{1,0:T(8,128)(2,1)} %get-tuple-element.22), channel_id=1, source_target_pairs={{0,14},{2,16},{4,18},{6,20},{8,22},{10,24},{12,26},{14,28},{16,30}... | collective-permute-start | bytes 147464 | tf_op jit(solution)/shard_map/ppermute | solution.py:19
  40.9 74.2 %collective-permute-start.2 = (bf16[384,64]{1,0:T(8,128)(2,1)}, bf16[384,64]{1,0:T(8,128)(2,1)}, u32[]{:S(2)}, u32[]{:S(2)}) collective-permute-start(bf16[384,64]{1,0:T(8,128)(2,1)} %get-tuple-element.21), channel_id=1, source_target_pairs={{0,12},{2,14},{4,16},{6,18},{8,20},{10,22},{12,24},{14,26},{16,28}... | collective-permute-start | bytes 147464 | tf_op jit(solution)/shard_map/ppermute | solution.py:19
  42.9 75.8 %collective-permute-start.3 = (bf16[384,64]{1,0:T(8,128)(2,1)}, bf16[384,64]{1,0:T(8,128)(2,1)}, u32[]{:S(2)}, u32[]{:S(2)}) collective-permute-start(bf16[384,64]{1,0:T(8,128)(2,1)} %get-tuple-element.20), channel_id=1, source_target_pairs={{0,10},{2,12},{4,14},{6,16},{8,18},{10,20},{12,22},{14,24},{16,26}... | collective-permute-start | bytes 147464 | tf_op jit(solution)/shard_map/ppermute | solution.py:19
  44.8 76.1 %collective-permute-start.4 = (bf16[384,64]{1,0:T(8,128)(2,1)}, bf16[384,64]{1,0:T(8,128)(2,1)}, u32[]{:S(2)}, u32[]{:S(2)}) collective-permute-start(bf16[384,64]{1,0:T(8,128)(2,1)} %get-tuple-element.19), channel_id=1, source_target_pairs={{0,8},{2,10},{4,12},{6,14},{8,16},{10,18},{12,20},{14,22},{16,24},... | collective-permute-start | bytes 147464 | tf_op jit(solution)/shard_map/ppermute | solution.py:19
  107.2 17.3 %copy-start.6 = (bf16[384,64]{1,0:T(8,128)(2,1)S(1)}, bf16[384,64]{1,0:T(8,128)(2,1)}, u32[]{:S(2)}) copy-start(bf16[384,64]{1,0:T(8,128)(2,1)} %get-tuple-element.12) | copy-start | bytes 147460
  107.2 18.6 %copy-start.5 = (bf16[384,64]{1,0:T(8,128)(2,1)S(1)}, bf16[384,64]{1,0:T(8,128)(2,1)}, u32[]{:S(2)}) copy-start(bf16[384,64]{1,0:T(8,128)(2,1)} %get-tuple-element.11) | copy-start | bytes 147460
  107.2 20.0 %copy-start.4 = (bf16[384,64]{1,0:T(8,128)(2,1)S(1)}, bf16[384,64]{1,0:T(8,128)(2,1)}, u32[]{:S(2)}) copy-start(bf16[384,64]{1,0:T(8,128)(2,1)} %get-tuple-element.10) | copy-start | bytes 147460
  107.3 47.0 %copy-start = (bf16[32,160,64]{2,1,0:T(8,128)(2,1)S(1)}, bf16[32,160,64]{2,1,0:T(8,128)(2,1)}, u32[]{:S(2)}) copy-start(bf16[32,160,64]{2,1,0:T(8,128)(2,1)} %copy.22) | copy-start | bytes 1966084
  109.9 13.2 %collective-permute-start.5 = (bf16[384,64]{1,0:T(8,128)(2,1)S(1)}, bf16[384,64]{1,0:T(8,128)(2,1)S(1)}, u32[]{:S(2)}, u32[]{:S(2)}) collective-permute-start(bf16[384,64]{1,0:T(8,128)(2,1)S(1)} %copy-done.12), channel_id=1, source_target_pairs={{0,6},{2,8},{4,10},{6,12},{8,14},{10,16},{12,18},{14,20},{16,22},{... | collective-permute-start | bytes 147464 | tf_op jit(solution)/shard_map/ppermute | solution.py:19
  112.2 12.3 %collective-permute-start.6 = (bf16[384,64]{1,0:T(8,128)(2,1)S(1)}, bf16[384,64]{1,0:T(8,128)(2,1)S(1)}, u32[]{:S(2)}, u32[]{:S(2)}) collective-permute-start(bf16[384,64]{1,0:T(8,128)(2,1)S(1)} %copy-done.11), channel_id=1, source_target_pairs={{0,4},{2,6},{4,8},{6,10},{8,12},{10,14},{12,16},{14,18},{16,20},{1... | collective-permute-start | bytes 147464 | tf_op jit(solution)/shard_map/ppermute | solution.py:19
  115.1 10.7 %collective-permute-start.7 = (bf16[384,64]{1,0:T(8,128)(2,1)S(1)}, bf16[384,64]{1,0:T(8,128)(2,1)S(1)}, u32[]{:S(2)}, u32[]{:S(2)}) collective-permute-start(bf16[384,64]{1,0:T(8,128)(2,1)S(1)} %copy-done.10), channel_id=1, source_target_pairs={{0,2},{2,4},{4,6},{6,8},{8,10},{10,12},{12,14},{14,16},{16,18},{18... | collective-permute-start | bytes 147464 | tf_op jit(solution)/shard_map/ppermute | solution.py:19
  118.7 8.5 %collective-permute-start.8 = (bf16[384,64]{1,0:T(8,128)(2,1)S(1)}, bf16[384,64]{1,0:T(8,128)(2,1)S(1)}, u32[]{:S(2)}, u32[]{:S(2)}) collective-permute-start(bf16[384,64]{1,0:T(8,128)(2,1)S(1)} %copy-done.9), channel_id=1, source_target_pairs={{2,0},{4,2},{6,4},{8,6},{10,8},{12,10},{14,12},{16,14},{18,16},{20... | collective-permute-start | bytes 147464 | tf_op jit(solution)/shard_map/ppermute | solution.py:19
  120.9 8.6 %collective-permute-start.9 = (bf16[384,64]{1,0:T(8,128)(2,1)S(1)}, bf16[384,64]{1,0:T(8,128)(2,1)S(1)}, u32[]{:S(2)}, u32[]{:S(2)}) collective-permute-start(bf16[384,64]{1,0:T(8,128)(2,1)S(1)} %copy-done.8), channel_id=1, source_target_pairs={{4,0},{6,2},{8,4},{10,6},{12,8},{14,10},{16,12},{18,14},{20,16},{2... | collective-permute-start | bytes 147464 | tf_op jit(solution)/shard_map/ppermute | solution.py:19
  123.2 9.2 %collective-permute-start.10 = (bf16[384,64]{1,0:T(8,128)(2,1)S(1)}, bf16[384,64]{1,0:T(8,128)(2,1)S(1)}, u32[]{:S(2)}, u32[]{:S(2)}) collective-permute-start(bf16[384,64]{1,0:T(8,128)(2,1)S(1)} %copy-done.7), channel_id=1, source_target_pairs={{6,0},{8,2},{10,4},{12,6},{14,8},{16,10},{18,12},{20,14},{22,16},{... | collective-permute-start | bytes 147464 | tf_op jit(solution)/shard_map/ppermute | solution.py:19
  124.5 11.4 %collective-permute-start.11 = (bf16[384,64]{1,0:T(8,128)(2,1)S(1)}, bf16[384,64]{1,0:T(8,128)(2,1)S(1)}, u32[]{:S(2)}, u32[]{:S(2)}) collective-permute-start(bf16[384,64]{1,0:T(8,128)(2,1)S(1)} %copy-done.6), channel_id=1, source_target_pairs={{8,0},{10,2},{12,4},{14,6},{16,8},{18,10},{20,12},{22,14},{24,16},... | collective-permute-start | bytes 147464 | tf_op jit(solution)/shard_map/ppermute | solution.py:19
  125.9 13.1 %collective-permute-start.12 = (bf16[384,64]{1,0:T(8,128)(2,1)S(1)}, bf16[384,64]{1,0:T(8,128)(2,1)S(1)}, u32[]{:S(2)}, u32[]{:S(2)}) collective-permute-start(bf16[384,64]{1,0:T(8,128)(2,1)S(1)} %copy-done.5), channel_id=1, source_target_pairs={{10,0},{12,2},{14,4},{16,6},{18,8},{20,10},{22,12},{24,14},{26,16}... | collective-permute-start | bytes 147464 | tf_op jit(solution)/shard_map/ppermute | solution.py:19
  127.2 14.5 %collective-permute-start.13 = (bf16[384,64]{1,0:T(8,128)(2,1)S(1)}, bf16[384,64]{1,0:T(8,128)(2,1)S(1)}, u32[]{:S(2)}, u32[]{:S(2)}) collective-permute-start(bf16[384,64]{1,0:T(8,128)(2,1)S(1)} %copy-done.4), channel_id=1, source_target_pairs={{12,0},{14,2},{16,4},{18,6},{20,8},{22,10},{24,12},{26,14},{28,16}... | collective-permute-start | bytes 147464 | tf_op jit(solution)/shard_map/ppermute | solution.py:19
  129.5 14.9 %collective-permute-start.14 = (bf16[384,64]{1,0:T(8,128)(2,1)S(1)}, bf16[384,64]{1,0:T(8,128)(2,1)S(1)}, u32[]{:S(2)}, u32[]{:S(2)}) collective-permute-start(bf16[384,64]{1,0:T(8,128)(2,1)S(1)} %get-tuple-element.9), channel_id=1, source_target_pairs={{14,0},{16,2},{18,4},{20,6},{22,8},{24,10},{26,12},{28,14},{30,16}... | collective-permute-start | bytes 147464 | tf_op jit(solution)/shard_map/ppermute | solution.py:19
  132.4 21.8 %collective-permute-start.15 = (bf16[384,64]{1,0:T(8,128)(2,1)S(1)}, bf16[384,64]{1,0:T(8,128)(2,1)S(1)}, u32[]{:S(2)}, u32[]{:S(2)}) collective-permute-start(bf16[384,64]{1,0:T(8,128)(2,1)S(1)} %get-tuple-element.8), channel_id=1, source_target_pairs={{16,0},{18,2},{20,4},{22,6},{24,8},{26,10},{28,12},{30,14},{17,1},... | collective-permute-start | bytes 147464 | tf_op jit(solution)/shard_map/ppermute | solution.py:19
  (7 other events, 74.5 us)
Sparse Core Ops, SparseCore 0:
  425.9 5.2 reduce-scatter.1

commit v2 on v1

--- a/solution.py
+++ b/solution.py
@@ -13,10 +13,14 @@
 BLANK = 16
 
 
-def passed_along(block, axis, distance):
-    devices = range(lax.axis_size(axis))
-    route = [(i - distance, i) for i in devices if i - distance in devices]
-    return lax.ppermute(block, axis, route)
+def side_by_side(blocks):
+    half = blocks.shape[1] // 2
+    return jnp.concatenate([blocks[:, :half], blocks[:, half:]], axis=2)
+
+
+def one_below_other(blocks):
+    half = blocks.shape[2] // 2
+    return jnp.concatenate([blocks[:, :, :half], blocks[:, :, half:]], axis=1)
 
 
 def gather_multiply(targets, chunk, steps, offset_ref, index_ref, table_ref, kernel_ref, out_ref, held_ref):
@@ -122,17 +126,34 @@
         j - reach_each if j < reach_each else j - reach_each + 1 for j in range(2 * reach_each)
     ]
     own = jnp.transpose(fine_multipole)
-    outgoing = jnp.take(own, send_list[0].reshape(-1), axis=0, mode="clip").reshape(
-        2 * reach_each, ghost_slots, width
+    sub = lax.axis_index("sub")
+    mine = lax.dynamic_slice_in_dim(send_list[0], sub * reach_each, reach_each, 0)
+    outgoing = jnp.take(own, mine.reshape(-1), axis=0, mode="clip").reshape(
+        reach_each, ghost_slots, width
     )
-    arrivals = [
-        passed_along(outgoing[j], "morton", -near_steps[j]) for j in range(2 * reach_each)
-    ]
+    outgoing = side_by_side(outgoing)
+    ranges, subs = lax.axis_size("morton"), lax.axis_size("sub")
+    arrivals = []
+    for k in range(reach_each):
+        route = [
+            (q * subs + s, (q - near_steps[s * reach_each + k]) * subs + s)
+            for q in range(ranges)
+            for s in range(subs)
+            if 0 <= q - near_steps[s * reach_each + k] < ranges
+        ]
+        arrivals.append(lax.ppermute(outgoing[k], ("morton", "sub"), route))
+    here = jnp.stack(arrivals)
+    there = lax.ppermute(here, "sub", [(0, 1), (1, 0)])
+    ghosts = jnp.concatenate(
+        [jnp.where(sub == 0, here, there), jnp.where(sub == 0, there, here)], axis=0
+    )
+    ghosts = one_below_other(ghosts).reshape(-1, width)
     coarse = lax.all_gather(
-        jnp.transpose(coarse_multipole), ("morton", "sub"), axis=0, tiled=True
+        side_by_side(jnp.transpose(coarse_multipole)[None]), ("morton", "sub"), axis=0, tiled=True
     )
+    coarse = one_below_other(coarse).reshape(-1, width)
     blank = jnp.zeros((BLANK, width), jnp.bfloat16)
-    rows = jnp.concatenate([own, *arrivals, blank, coarse, blank], axis=0)
+    rows = jnp.concatenate([own, ghosts, blank, coarse, blank], axis=0)
     rows = rows.astype(jnp.float32)
     table = jnp.concatenate([rows, rows], axis=1)[:, None, :]
     no_source = own.shape[0] + 2 * reach_each * ghost_slots

time: 443 us -> 409 us (0.923)
  waiting for transfers between devices: 28.4 us -> 11 us
  starting transfers between devices: 34.6 us -> 25.3 us
  local copies, waits for them, and re-layouts: 51.8 us -> 44.8 us
    ppermute x16 -> x9, waiting for transfers between devices: 23 us -> 1.33 us  [the longest x1 1.31 us: per_device(): there = lax.ppermute(here, 'sub', [(0, 1), (1, 0)])]
    ppermute x16 -> x9, starting transfers between devices: 34.6 us -> 25.3 us  [the longest x8 24.1 us: per_device(): arrivals.append(lax.ppermute(outgoing[k], ('morton', 'sub'), route))]
    gather x1, local copies, waits for them, and re-layouts: 18.1 us -> 9.16 us  [per_device(): jnp.take(own, mine.reshape(-1), axis=0, mode='clip')]
    unnamed x51 -> x26, local copies, waits for them, and re-layouts: 15.4 us -> 14.8 us
  transfers between devices with their start and end apart: 17 -> 10, of which waited for: 8 -> 2; matrix products, arithmetic and copies ran while one was open for 6% -> 8% of each run, Pallas kernels for 0% -> 0%
where the time goes in v2:
time: 409 us; the launch traced here: 408 us
  Pallas kernels  268 us (66%)
  local copies, waits for them, and re-layouts  44.8 us (11%)
  blocking collectives  38.9 us (10%)
  starting transfers between devices  25.3 us (6%)
  between operations  14.3 us (3%)
  waiting for transfers between devices  11 us (3%)
  other arithmetic  6.43 us (2%)
    pallas_call x1, Pallas kernels, translate(): pl.pallas_call(functools.partial(gather_multiply, targets, chunk, steps),...  268 us
    all_gather x1, blocking collectives, per_device(): lax.all_gather(side_by_side(jnp.transpose(coarse_multipole)[None]), ('mor...  38.9 us
    ppermute x8, starting transfers between devices, per_device(): arrivals.append(lax.ppermute(outgoing[k], ('morton', 'sub'), route))  24.1 us
    unnamed x26, local copies, waits for them, and re-layouts  14.8 us
    reduce_scatter x1, waiting for transfers between devices, per_device(): local = lax.psum_scatter(part, 'sub', scatter_dimension=0, tiled=True)  9.61 us
    gather x1, local copies, waits for them, and re-layouts, per_device(): jnp.take(own, mine.reshape(-1), axis=0, mode='clip')  9.16 us
  transfers between devices with their start and end apart: 10, of which 2 were waited for; matrix products, arithmetic and copies ran while one was open for 8% of the time, Pallas kernels for 0%

profile of v2, /device:TPU:0, one launch (start us, length us, event | category | flops | bytes accessed | tf_op | source)
XLA Modules:
  0.0 408.3 jit_solution(11898851802165305356)
XLA Ops:
  7.9 1.2 copy.21
  9.2 9.2 %gather_fusion = bf16[3072,64]{1,0:T(8,128)(2,1)S(1)} fusion(bf16[2048,64]{1,0:T(8,128)(2,1)S(1)} %bitcast.46, s32[3072]{0:T(1024)S(1)} %broadcast_clamp_fusion), kind=kCustom, calls=%fused_computation | custom fusion | bytes 798720 | tf_op jit(solution)/shard_map/jit(_take)/gather | solution.py:131
  19.3 6.7 %collective-permute-start = (bf16[192,128]{1,0:T(8,128)(2,1)}, bf16[192,128]{1,0:T(8,128)(2,1)}, u32[]{:S(2)}, u32[]{:S(2)}) collective-permute-start(bf16[192,128]{1,0:T(8,128)(2,1)} %get-tuple-element.13), channel_id=1, source_target_pairs={{0,16},{2,18},{3,1},{4,20},{5,3},{6,22},{7,5},{8,24},{9,7},{10,26}... | collective-permute-start | bytes 147464 | tf_op jit(solution)/shard_map/ppermute | solution.py:144
  26.0 6.0 %collective-permute-start.1 = (bf16[192,128]{1,0:T(8,128)(2,1)}, bf16[192,128]{1,0:T(8,128)(2,1)}, u32[]{:S(2)}, u32[]{:S(2)}) collective-permute-start(bf16[192,128]{1,0:T(8,128)(2,1)} %get-tuple-element.14), channel_id=1, source_target_pairs={{0,14},{2,16},{4,18},{5,1},{6,20},{7,3},{8,22},{9,5},{10,24},{11,7... | collective-permute-start | bytes 147464 | tf_op jit(solution)/shard_map/ppermute | solution.py:144
  32.0 1.9 collective-permute-start.2
  33.9 1.9 collective-permute-start.3
  35.8 1.9 collective-permute-start.4
  37.9 38.9 %all_gather.3 = bf16[32,80,128]{2,1,0:T(8,128)(2,1)S(1)} all-gather(bf16[1,80,128]{2,1,0:T(8,128)(2,1)S(1)} %pad_maximum_fusion.3), channel_id=1, replica_groups=mesh['morton'=16,'sub'=2] {'morton','sub'}, dimensions={0}, use_global_device_ids=true | all-gather | bytes 675840 | tf_op jit(solution)/shard_map/all_gather | solution.py:151
  77.0 1.2 fusion.16
  79.3 1.7 concatenate.25
  80.9 1.3 pad.8
  82.2 3.5 reshape.26
  85.7 4.3 %copy.20 = s32[40,37,4,64]{3,2,1,0:T(4,128)} copy(s32[40,37,4,64]{3,1,2,0:T(8,128)} %bitcast.48) | data formatting | bytes 3031040 | tf_op jit(solution)/shard_map/transpose | solution.py:93
  90.1 4.2 %reshape.27.index_ref = s32[40,37,1,256]{3,2,1,0:T(1,128)S(1)} reshape(s32[40,37,4,64]{3,2,1,0:T(4,128)} %copy.20) | data formatting | bytes 3031040 | tf_op jit(solution)/shard_map/reshape | solution.py:94
  94.2 6.7 %copy.26 = bf16[158,64,64]{2,1,0:T(8,128)(2,1)} copy(bf16[158,64,64]{0,1,2:T(8,128)(2,1)} %bitcast.52) | data formatting | bytes 2588672
  101.0 2.5 pad.9.clone
  103.5 1.3 collective-permute-start.5
  105.6 1.3 collective-permute-start.6
  107.7 3.2 collective-permute-start.7
  113.4 1.2 collective-permute-start.8
  114.6 1.3 collective-permute-done.8
  117.0 3.7 maximum_convert_fusion
  120.7 267.6 %shard_map.77 = f32[2368,64]{1,0:T(8,128)} custom-call(s32[8]{0:T(128)S(1)} %iota.3.offset_ref, s32[40,37,1,256]{3,2,1,0:T(1,128)S(1)} %reshape.27.index_ref, f32[13344,1,128]{2,1,0:T(1,128)} %bitcast.47, bf16[40,256,64]{2,1,0:T(8,128)(2,1)S(1)} %bitcast.45), custom_call_target="tpu_custom_call" | custom-call | tf_op jit(solution)/shard_map/pallas_call | solution.py:95
  388.3 9.6 %reduce-scatter.2.cloned.1.call-done = f32[1184,64]{1,0:T(8,128)} async-done(((f32[2368,64]{1,0:T(8,128)}), f32[1184,64]{1,0:T(8,128)}) %reduce-scatter.2.cloned.1.call-update) | async-done | bytes 303120 | tf_op jit(solution)/shard_map/reduce_scatter | solution.py:175
  (53 shorter events, 11.9 us)
Async XLA Ops:
  7.2 0.7 copy-start
  7.2 390.7 %reduce-scatter.2.cloned.1.call-start = ((), (), s32[]{:S(2)}) async-start(), calls=%async_computation.1 | async-start | bytes 1818624 | tf_op jit(solution)/shard_map/reduce_scatter | solution.py:175
  9.2 28.5 %copy-start.4 = (bf16[64,160]{1,0:T(8,128)(2,1)S(1)}, bf16[64,160]{1,0:T(8,128)(2,1)}, u32[]{:S(2)}) copy-start(bf16[64,160]{1,0:T(8,128)(2,1)} %param.7) | copy-start | bytes 61444
  18.3 58.7 %copy-start.1 = (s32[158,2048]{1,0:T(8,128)S(1)}, s32[158,2048]{1,0:T(8,128)}, u32[]{:S(2)}) copy-start(s32[158,2048]{1,0:T(8,128)} %param.10) | copy-start | bytes 3883012
  19.3 58.9 %copy-start.2 = (s32[158,320]{1,0:T(8,128)S(1)}, s32[158,320]{1,0:T(8,128)}, u32[]{:S(2)}) copy-start(s32[158,320]{1,0:T(8,128)} %param.11) | copy-start | bytes 606724
  19.3 84.2 %collective-permute-start = (bf16[192,128]{1,0:T(8,128)(2,1)}, bf16[192,128]{1,0:T(8,128)(2,1)}, u32[]{:S(2)}, u32[]{:S(2)}) collective-permute-start(bf16[192,128]{1,0:T(8,128)(2,1)} %get-tuple-element.13), channel_id=1, source_target_pairs={{0,16},{2,18},{3,1},{4,20},{5,3},{6,22},{7,5},{8,24},{9,7},{10,26}... | collective-permute-start | bytes 147464 | tf_op jit(solution)/shard_map/ppermute | solution.py:144
  26.0 79.6 %collective-permute-start.1 = (bf16[192,128]{1,0:T(8,128)(2,1)}, bf16[192,128]{1,0:T(8,128)(2,1)}, u32[]{:S(2)}, u32[]{:S(2)}) collective-permute-start(bf16[192,128]{1,0:T(8,128)(2,1)} %get-tuple-element.14), channel_id=1, source_target_pairs={{0,14},{2,16},{4,18},{5,1},{6,20},{7,3},{8,22},{9,5},{10,24},{11,7... | collective-permute-start | bytes 147464 | tf_op jit(solution)/shard_map/ppermute | solution.py:144
  32.0 75.7 %collective-permute-start.2 = (bf16[192,128]{1,0:T(8,128)(2,1)}, bf16[192,128]{1,0:T(8,128)(2,1)}, u32[]{:S(2)}, u32[]{:S(2)}) collective-permute-start(bf16[192,128]{1,0:T(8,128)(2,1)} %get-tuple-element.15), channel_id=1, source_target_pairs={{0,12},{2,14},{4,16},{6,18},{7,1},{8,20},{9,3},{10,22},{11,5},{12,... | collective-permute-start | bytes 147464 | tf_op jit(solution)/shard_map/ppermute | solution.py:144
  33.9 77.9 %collective-permute-start.3 = (bf16[192,128]{1,0:T(8,128)(2,1)}, bf16[192,128]{1,0:T(8,128)(2,1)}, u32[]{:S(2)}, u32[]{:S(2)}) collective-permute-start(bf16[192,128]{1,0:T(8,128)(2,1)} %get-tuple-element.16), channel_id=1, source_target_pairs={{0,10},{2,12},{4,14},{6,16},{8,18},{9,1},{10,20},{11,3},{12,22},{1... | collective-permute-start | bytes 147464 | tf_op jit(solution)/shard_map/ppermute | solution.py:144
  35.8 76.8 %collective-permute-start.4 = (bf16[192,128]{1,0:T(8,128)(2,1)}, bf16[192,128]{1,0:T(8,128)(2,1)}, u32[]{:S(2)}, u32[]{:S(2)}) collective-permute-start(bf16[192,128]{1,0:T(8,128)(2,1)} %get-tuple-element.17), channel_id=1, source_target_pairs={{0,8},{2,10},{4,12},{6,14},{8,16},{10,18},{11,1},{12,20},{13,3},{1... | collective-permute-start | bytes 147464 | tf_op jit(solution)/shard_map/ppermute | solution.py:144
  101.0 2.5 copy-start.3
  103.5 9.9 %collective-permute-start.5 = (bf16[192,128]{1,0:T(8,128)(2,1)S(1)}, bf16[192,128]{1,0:T(8,128)(2,1)S(1)}, u32[]{:S(2)}, u32[]{:S(2)}) collective-permute-start(bf16[192,128]{1,0:T(8,128)(2,1)S(1)} %copy-done.3), channel_id=1, source_target_pairs={{0,6},{2,8},{4,10},{6,12},{8,14},{10,16},{12,18},{13,1},{14,20},{1... | collective-permute-start | bytes 147464 | tf_op jit(solution)/shard_map/ppermute | solution.py:144
  105.6 7.8 %collective-permute-start.6 = (bf16[192,128]{1,0:T(8,128)(2,1)S(1)}, bf16[192,128]{1,0:T(8,128)(2,1)S(1)}, u32[]{:S(2)}, u32[]{:S(2)}) collective-permute-start(bf16[192,128]{1,0:T(8,128)(2,1)S(1)} %get-tuple-element.19), channel_id=1, source_target_pairs={{0,4},{2,6},{4,8},{6,10},{8,12},{10,14},{12,16},{14,18},{15,1},{16... | collective-permute-start | bytes 147464 | tf_op jit(solution)/shard_map/ppermute | solution.py:144
  107.7 5.7 %collective-permute-start.7 = (bf16[192,128]{1,0:T(8,128)(2,1)S(1)}, bf16[192,128]{1,0:T(8,128)(2,1)S(1)}, u32[]{:S(2)}, u32[]{:S(2)}) collective-permute-start(bf16[192,128]{1,0:T(8,128)(2,1)S(1)} %get-tuple-element.12), channel_id=1, source_target_pairs={{0,2},{2,4},{4,6},{6,8},{8,10},{10,12},{12,14},{14,16},{16,18},{17... | collective-permute-start | bytes 147464 | tf_op jit(solution)/shard_map/ppermute | solution.py:144
  113.4 2.5 collective-permute-start.8
Sparse Core Ops, SparseCore 0:
  388.4 9.4 reduce-scatter.1
